TPU v7x, 32 devices: a whole 2x2x4 slice. The times are simulated.
32 devices in a mesh: row: 4 (over y, x), col: 4 (over z), rep: 2 (over core).
Axes of the slice: x: 2, y: 2, z: 4, core: 2. Of those that a mesh axis runs over, the one named last changes fastest.
Arguments:
- features: bfloat16 [2, 2048, 512], P('rep', ('row', 'col')), may hold values from -6 to 6
- cotangent: bfloat16 [2, 2048, 512], P('rep', ('row', 'col')), may hold values from -6 to 6
- weight: bfloat16 [512, 512], replicated, may hold values from -0.25 to 0.25
- tile_values: bfloat16 [2, 256, 128, 128], P('rep', ('row', 'col')), may hold values from -0.25 to 0.25
- tile_out: int32 [2, 256], P('rep', ('row', 'col')), may hold values from 0 to 3
- tile_in: int32 [2, 256], P('rep', ('row', 'col')), may hold values from 0 to 3
- tile_count: int32 [2, 16], P('rep', ('row', 'col')), may hold values from 8 to 16, as said below
Outputs:
- out_feats: bfloat16 [2, 2048, 512], P('rep', ('row', 'col'))
- grad_feats: bfloat16 [2, 2048, 512], P('rep', ('row', 'col'))
- grad_weight: float32 [512, 512], replicated
Inputs may be any that keep to these rules, and one draw needn't show every extreme that they name: `tile_count`: in each window some group has all 16 slots live.
All inputs are finite; a program needn't handle non-finite values.
Results may differ from a plain program's by a relative error of at most 0.015.
Values may be sent and summed in bfloat16 or wider, within the bound.
A program may use at most 64 MiB of HBM per device.

v0:
```python
import jax
import jax.numpy as jnp
from jax import lax
from jax.sharding import PartitionSpec as P

SECTIONS = 4


def passed_along(value, axis, steps):
    count = lax.axis_size(axis)
    leading, last = (max(0, -steps), min(count, count - steps))
    return lax.ppermute(value, axis, [(source, source + steps) for source in range(leading, last)])


def body(features, cotangent, weight, tile_values, tile_out, tile_in, tile_count):
    field_in = features[0]
    values = tile_values[0]
    outs_idx = tile_out[0]
    ins_idx = tile_in[0]
    count = tile_count[0, 0]
    node_rows, width = field_in.shape
    edge = values.shape[-1]
    per_span = node_rows // edge
    half = SECTIONS // 2
    col_count = lax.axis_size("col")
    out_count = col_count * per_span
    in_count = SECTIONS * per_span
    slot_total = values.shape[0]
    live = (jnp.arange(slot_total, dtype=jnp.int32) < count).astype(jnp.float32)
    out_hot = (outs_idx[None, :] == jnp.arange(out_count, dtype=jnp.int32)[:, None]).astype(
        jnp.float32
    ) * live[None, :]
    in_hot = (ins_idx[None, :] == jnp.arange(in_count, dtype=jnp.int32)[:, None]).astype(
        jnp.float32
    ) * live[None, :]
    pieces = []
    for section in range(SECTIONS):
        offset = section - half
        if offset == 0:
            pieces.append(field_in)
        else:
            pieces.append(passed_along(field_in, "row", -offset))
    blocks = jnp.stack(pieces)
    picked = blocks[ins_idx]
    prods = jnp.einsum("tij,tjf->tif", values, picked, preferred_element_type=jnp.float32)
    part = jnp.einsum("ot,tif->oif", out_hot, prods, precision=lax.Precision.HIGHEST)
    summed = lax.psum_scatter(
        part.reshape(out_count * edge, width).astype(jnp.bfloat16),
        "col",
        scatter_dimension=0,
        tiled=True,
    )
    pre = jnp.dot(summed, weight, preferred_element_type=jnp.float32)
    out_feats = jax.nn.silu(pre).astype(jnp.bfloat16)
    sigma = jax.nn.sigmoid(pre)
    dpre = (cotangent[0].astype(jnp.float32) * sigma * (1.0 + pre * (1.0 - sigma))).astype(
        jnp.bfloat16
    )
    local_grad = jnp.einsum("nf,ng->fg", summed, dpre, preferred_element_type=jnp.float32)
    total_nodes = node_rows * lax.axis_size("row") * col_count * lax.axis_size("rep")
    grad_weight = lax.psum(local_grad, ("row", "col", "rep")) * jnp.float32(total_nodes) ** (-0.5)
    dhidden = jnp.einsum("nf,gf->ng", dpre, weight, preferred_element_type=jnp.float32).astype(
        jnp.bfloat16
    )
    row_grads = lax.all_gather(dhidden, "col", axis=0, tiled=True).reshape(out_count, edge, width)
    chosen = row_grads[outs_idx]
    back_prods = jnp.einsum("tij,tif->tjf", values, chosen, preferred_element_type=jnp.float32)
    sections_part = jnp.einsum("it,tjf->ijf", in_hot, back_prods, precision=lax.Precision.HIGHEST)
    sections_part = sections_part.astype(jnp.bfloat16)
    total = jnp.zeros((node_rows, width), jnp.float32)
    for section in range(SECTIONS):
        offset = section - half
        if offset == 0:
            arrived = sections_part[section]
        else:
            arrived = passed_along(sections_part[section], "row", offset)
        total = total + arrived.astype(jnp.float32)
    grad_feats = total.astype(jnp.bfloat16)
    return (out_feats[None], grad_feats[None], grad_weight)


def solution(mesh):
    return jax.shard_map(
        body,
        mesh=mesh,
        in_specs=(
            P("rep", ("row", "col"), None),
            P("rep", ("row", "col"), None),
            P(),
            P("rep", ("row", "col"), None, None),
            P("rep", ("row", "col")),
            P("rep", ("row", "col")),
            P("rep", ("row", "col")),
        ),
        out_specs=(P("rep", ("row", "col"), None), P("rep", ("row", "col"), None), P()),
        check_vma=False,
    )
```

profile of v0, /device:TPU:0, one launch (start us, length us, event | category | flops | bytes accessed | tf_op | source)
XLA Modules:
  0.0 224.5 jit_solution(10835809086337116893)
XLA Ops:
  7.2 5.0 %collective-permute-start = (bf16[128,512]{1,0:T(8,128)(2,1)}, bf16[128,512]{1,0:T(8,128)(2,1)S(1)}, u32[]{:S(2)}, u32[]{:S(2)}) collective-permute-start(bf16[128,512]{1,0:T(8,128)(2,1)} %bitcast.76), channel_id=1, source_target_pairs={{0,16},{8,24},{1,17},{9,25},{2,18},{10,26},{3,19},{11,27},{4,20},{... | collective-permute-start | bytes 393224 | tf_op jit(solution)/shard_map/ppermute | solution.py:12
  12.2 3.4 %collective-permute-start.1 = (bf16[128,512]{1,0:T(8,128)(2,1)}, bf16[128,512]{1,0:T(8,128)(2,1)S(1)}, u32[]{:S(2)}, u32[]{:S(2)}) collective-permute-start(bf16[128,512]{1,0:T(8,128)(2,1)} %bitcast.77), channel_id=1, source_target_pairs={{0,8},{8,16},{16,24},{1,9},{9,17},{17,25},{2,10},{10,18},{18,26},{... | collective-permute-start | bytes 393224 | tf_op jit(solution)/shard_map/ppermute | solution.py:12
  15.7 1.3 collective-permute-start.2
  18.5 4.3 %collective-permute-done.2 = bf16[128,512]{1,0:T(8,128)(2,1)S(1)} collective-permute-done((bf16[128,512]{1,0:T(8,128)(2,1)}, bf16[128,512]{1,0:T(8,128)(2,1)S(1)}, u32[]{:S(2)}, u32[]{:S(2)}) %collective-permute-start.2) | collective-permute-done | bytes 131104 | tf_op jit(solution)/shard_map/ppermute | solution.py:12
  22.7 1.0 pad_maximum_fusion
  24.4 2.7 %fusion.12 = f32[16,512,128]{2,1,0:T(8,128)} fusion(bf16[16,128,512]{2,1,0:T(8,128)(2,1)S(1)} %gather_fusion, bf16[1,16,128,128]{3,2,1,0:T(8,128)(2,1)S(1)} %copy-done), kind=kOutput, calls=%fused_computation.12 | convolution fusion | flops 268435456 | bytes 6815744 | tf_op jit(solution)/shard_map/tij,tjf->tif/dot_general | solution.py:45
  27.1 5.5 %copy.16 = f32[16,512,128]{1,0,2:T(8,128)} copy(f32[16,512,128]{2,1,0:T(8,128)} %fusion.12) | data formatting | bytes 8388608 | tf_op jit(solution)/shard_map/tij,tjf->tif/dot_general | solution.py:45
  32.6 4.3 %fusion.4 = bf16[4,128,512]{2,0,1:T(4,128)(2,1)S(1)} fusion(f32[16,512,128]{1,0,2:T(8,128)} %copy.16, f32[16]{0:T(128)S(1)} %compare_convert_fusion, s32[16]{0:T(128)S(1)} %bitcast.82), kind=kOutput, calls=%fused_computation.6 | convolution fusion | flops 50593920 | bytes 4718720 | tf_op jit(solution)/shard_map/ot,tif->oif/dot_general | solution.py:46
  37.0 0.9 copy.13
  38.0 21.4 %reduce-scatter.2.cloned.1.call-done = bf16[128,512]{1,0:T(8,128)(2,1)} async-done(((bf16[512,512]{1,0:T(8,128)(2,1)}), bf16[128,512]{1,0:T(8,128)(2,1)}) %reduce-scatter.2.cloned.1.call-update) | async-done | bytes 131088 | tf_op jit(solution)/shard_map/reduce_scatter | solution.py:47
  59.4 1.1 fusion.38
  60.9 15.9 %all_gather.3 = bf16[512,512]{1,0:T(8,128)(2,1)S(1)} all-gather(bf16[128,512]{1,0:T(8,128)(2,1)S(1)} %convolution_convert_fusion), channel_id=1, replica_groups=mesh['row'=4,'col'=4,'rep'=2] {'col'}, dimensions={0}, use_global_device_ids=true | all-gather | bytes 655360 | tf_op jit(solution)/shard_map/all_gather | solution.py:65
  77.4 2.8 %fusion.10 = f32[16,512,128]{2,1,0:T(8,128)} fusion(bf16[16,128,512]{2,1,0:T(8,128)(2,1)S(1)} %gather_fusion.1, bf16[1,16,128,128]{3,2,1,0:T(8,128)(2,1)S(1)} %copy-done), kind=kOutput, calls=%fused_computation.10 | convolution fusion | flops 268435456 | bytes 6815744 | tf_op jit(solution)/shard_map/tij,tif->tjf/dot_general | solution.py:67
  80.2 5.5 %copy.17 = f32[16,512,128]{1,0,2:T(8,128)} copy(f32[16,512,128]{2,1,0:T(8,128)} %fusion.10) | data formatting | bytes 8388608 | tf_op jit(solution)/shard_map/tij,tif->tjf/dot_general | solution.py:67
  85.7 1.4 fusion.34
  87.1 4.3 %fusion.7 = bf16[4,128,512]{2,0,1:T(4,128)(2,1)S(1)} fusion(f32[16,512,128]{1,0,2:T(8,128)} %copy.17, s32[16]{0:T(128)S(1)} %bitcast.83, f32[16]{0:T(128)S(1)} %compare_convert_fusion), kind=kOutput, calls=%fused_computation.7 | convolution fusion | flops 50593920 | bytes 4718720 | tf_op jit(solution)/shard_map/it,tjf->ijf/dot_general | solution.py:68
  91.4 0.7 fusion.37
  92.1 1.3 collective-permute-start.3
  93.5 1.3 collective-permute-start.4
  94.8 4.6 %collective-permute-start.5 = (bf16[128,512]{1,0:T(8,128)(2,1)S(1)}, bf16[128,512]{1,0:T(8,128)(2,1)S(1)}, u32[]{:S(2)}, u32[]{:S(2)}) collective-permute-start(bf16[128,512]{1,0:T(8,128)(2,1)S(1)} %bitcast.75), channel_id=1, source_target_pairs={{0,8},{8,16},{16,24},{1,9},{9,17},{17,25},{2,10},{10,18},{18,26},{... | collective-permute-start | bytes 393224 | tf_op jit(solution)/shard_map/ppermute | solution.py:12
  99.4 0.7 fusion.19
  100.3 1.7 collective-permute-done.5
  102.7 112.6 %all-reduce.2.cloned.1.call-done = f32[512,512]{1,0:T(8,128)} async-done(((f32[512,512]{1,0:T(8,128)}), f32[512,512]{1,0:T(8,128)}) %all-reduce.2.cloned.1.call-update) | async-done | bytes 1048592 | tf_op jit(solution)/shard_map/psum | solution.py:61
  215.3 2.3 %broadcast_multiply_fusion = f32[512,512]{1,0:T(8,128)} fusion(f32[512,512]{1,0:T(8,128)} %all-reduce.2.cloned.1.call-done), kind=kLoop, calls=%fused_computation.14 | loop fusion | flops 262144 | bytes 2097152 | tf_op jit(solution)/shard_map/mul | solution.py:61
  (32 shorter events, 3.7 us)
Async XLA Ops:
  7.2 17.2 %copy-start = (bf16[1,16,128,128]{3,2,1,0:T(8,128)(2,1)S(1)}, bf16[1,16,128,128]{3,2,1,0:T(8,128)(2,1)}, u32[]{:S(2)}) copy-start(bf16[1,16,128,128]{3,2,1,0:T(8,128)(2,1)} %param.10) | copy-start | bytes 1572868
  7.2 52.2 %reduce-scatter.2.cloned.1.call-start = ((), (), s32[]{:S(2)}) async-start(), calls=%async_computation.1 | async-start | bytes 655360 | tf_op jit(solution)/shard_map/reduce_scatter | solution.py:47
  7.2 11.1 %collective-permute-start = (bf16[128,512]{1,0:T(8,128)(2,1)}, bf16[128,512]{1,0:T(8,128)(2,1)S(1)}, u32[]{:S(2)}, u32[]{:S(2)}) collective-permute-start(bf16[128,512]{1,0:T(8,128)(2,1)} %bitcast.76), channel_id=1, source_target_pairs={{0,16},{8,24},{1,17},{9,25},{2,18},{10,26},{3,19},{11,27},{4,20},{... | collective-permute-start | bytes 393224 | tf_op jit(solution)/shard_map/ppermute | solution.py:12
  12.2 6.2 %collective-permute-start.1 = (bf16[128,512]{1,0:T(8,128)(2,1)}, bf16[128,512]{1,0:T(8,128)(2,1)S(1)}, u32[]{:S(2)}, u32[]{:S(2)}) collective-permute-start(bf16[128,512]{1,0:T(8,128)(2,1)} %bitcast.77), channel_id=1, source_target_pairs={{0,8},{8,16},{16,24},{1,9},{9,17},{17,25},{2,10},{10,18},{18,26},{... | collective-permute-start | bytes 393224 | tf_op jit(solution)/shard_map/ppermute | solution.py:12
  15.7 7.1 %collective-permute-start.2 = (bf16[128,512]{1,0:T(8,128)(2,1)}, bf16[128,512]{1,0:T(8,128)(2,1)S(1)}, u32[]{:S(2)}, u32[]{:S(2)}) collective-permute-start(bf16[128,512]{1,0:T(8,128)(2,1)} %bitcast.78), channel_id=1, source_target_pairs={{8,0},{16,8},{24,16},{9,1},{17,9},{25,17},{10,2},{18,10},{26,18},{... | collective-permute-start | bytes 393224 | tf_op jit(solution)/shard_map/ppermute | solution.py:12
  27.1 5.5 %copy-start.3 = (s32[1,16]{1,0:T(1,128)S(1)}, s32[1,16]{1,0:T(1,128)}, u32[]{:S(2)}) copy-start(s32[1,16]{1,0:T(1,128)} %param.11) | copy-start | bytes 196
  32.6 26.8 %copy-start.1 = (bf16[512,512]{1,0:T(8,128)(2,1)S(1)}, bf16[512,512]{1,0:T(8,128)(2,1)}, u32[]{:S(2)}) copy-start(bf16[512,512]{1,0:T(8,128)(2,1)} %param.9) | copy-start | bytes 1572868
  37.0 23.6 %copy-start.5 = (bf16[1,128,512]{2,1,0:T(8,128)(2,1)S(1)}, bf16[1,128,512]{2,1,0:T(8,128)(2,1)}, u32[]{:S(2)}) copy-start(bf16[1,128,512]{2,1,0:T(8,128)(2,1)} %param.8) | copy-start | bytes 393220
  37.9 177.4 %all-reduce.2.cloned.1.call-start = ((), (), s32[]{:S(2)}) async-start(), calls=%async_computation.2 | async-start | bytes 2097152 | tf_op jit(solution)/shard_map/psum | solution.py:61
  80.2 5.5 %copy-start.2 = (bf16[128,512]{1,0:T(8,128)(2,1)S(1)}, bf16[128,512]{1,0:T(8,128)(2,1)}, u32[]{:S(2)}) copy-start(bf16[128,512]{1,0:T(8,128)(2,1)} %reduce-scatter.2.cloned.1.call-done) | copy-start | bytes 393220
  85.7 1.4 copy-start.4
  92.1 8.0 %collective-permute-start.3 = (bf16[128,512]{1,0:T(8,128)(2,1)S(1)}, bf16[128,512]{1,0:T(8,128)(2,1)S(1)}, u32[]{:S(2)}, u32[]{:S(2)}) collective-permute-start(bf16[128,512]{1,0:T(8,128)(2,1)S(1)} %bitcast.73), channel_id=1, source_target_pairs={{16,0},{24,8},{17,1},{25,9},{18,2},{26,10},{19,3},{27,11},{20,4},{... | collective-permute-start | bytes 393224 | tf_op jit(solution)/shard_map/ppermute | solution.py:12
  93.5 6.9 %collective-permute-start.4 = (bf16[128,512]{1,0:T(8,128)(2,1)S(1)}, bf16[128,512]{1,0:T(8,128)(2,1)S(1)}, u32[]{:S(2)}, u32[]{:S(2)}) collective-permute-start(bf16[128,512]{1,0:T(8,128)(2,1)S(1)} %bitcast.74), channel_id=1, source_target_pairs={{8,0},{16,8},{24,16},{9,1},{17,9},{25,17},{10,2},{18,10},{26,18},{... | collective-permute-start | bytes 393224 | tf_op jit(solution)/shard_map/ppermute | solution.py:12
  94.8 7.2 %collective-permute-start.5 = (bf16[128,512]{1,0:T(8,128)(2,1)S(1)}, bf16[128,512]{1,0:T(8,128)(2,1)S(1)}, u32[]{:S(2)}, u32[]{:S(2)}) collective-permute-start(bf16[128,512]{1,0:T(8,128)(2,1)S(1)} %bitcast.75), channel_id=1, source_target_pairs={{0,8},{8,16},{16,24},{1,9},{9,17},{17,25},{2,10},{10,18},{18,26},{... | collective-permute-start | bytes 393224 | tf_op jit(solution)/shard_map/ppermute | solution.py:12
Sparse Core Ops, SparseCore 0:
  38.0 21.3 reduce-scatter.1
  87.2 128.0 all-reduce.1
where the time goes:
time: 225 us; the launch traced here: 224 us
  waiting for transfers between devices  140 us (62%)
  starting transfers between devices  16.9 us (8%)
  matrix products  16.9 us (8%)
  blocking collectives  15.9 us (7%)
  between operations  14.9 us (7%)
  local copies, waits for them, and re-layouts  13.4 us (6%)
  other arithmetic  6.11 us (3%)
    psum x1, waiting for transfers between devices, body(): lax.psum(local_grad, ('row', 'col', 'rep'))  113 us
    reduce_scatter x1, waiting for transfers between devices, body(): lax.psum_scatter(part.reshape(out_count * edge, width).astype(jnp.bfloat1...  21.4 us
    ppermute x6, starting transfers between devices, passed_along(): lax.ppermute(value, axis, [(source, source + steps) for source in range(l...  16.8 us
    all_gather x1, blocking collectives, body(): lax.all_gather(dhidden, 'col', axis=0, tiled=True)  15.9 us
    ppermute x6, waiting for transfers between devices, passed_along(): lax.ppermute(value, axis, [(source, source + steps) for source in range(l...  6.33 us
    dot_general x1, local copies, waits for them, and re-layouts, body(): jnp.einsum('tij,tif->tjf', values, chosen, preferred_element_type=jnp.flo...  5.54 us
    dot_general x1, local copies, waits for them, and re-layouts, body(): jnp.einsum('tij,tjf->tif', values, picked, preferred_element_type=jnp.flo...  5.51 us
  transfers between devices with their start and end apart: 8, of which 6 were waited for; matrix products, arithmetic and copies ran while one was open for 3% of the time, Pallas kernels for 0%

commit v1 on v0

--- a/solution.py
+++ b/solution.py
@@ -1,9 +1,28 @@
+import functools
 import jax
 import jax.numpy as jnp
 from jax import lax
 from jax.sharding import PartitionSpec as P
 
 SECTIONS = 4
+
+
+def watch_the_waves(z_in, axis_tag):
+    earlier, shaped = (lax.axis_size(axis_tag), lax.axis_index(axis_tag))
+    u_next, step_out = (z_in, 1)
+    while step_out < earlier:
+        runs = []
+        for k0 in range(earlier):
+            runs.append((k0, k0 ^ step_out))
+        field_out = lax.ppermute(u_next, axis_tag, runs)
+        h_now = jnp.concatenate([u_next, field_out], 0)
+        part_now = jnp.concatenate([field_out, u_next], 0)
+        u_next = jnp.where(shaped & step_out == 0, h_now, part_now)
+        step_out = 2 * step_out
+    return u_next
+
+
+clear_samples_all_on = functools.partial(watch_the_waves, axis_tag="col")
 
 
 def passed_along(value, axis, steps):
@@ -62,7 +81,7 @@
     dhidden = jnp.einsum("nf,gf->ng", dpre, weight, preferred_element_type=jnp.float32).astype(
         jnp.bfloat16
     )
-    row_grads = lax.all_gather(dhidden, "col", axis=0, tiled=True).reshape(out_count, edge, width)
+    row_grads = clear_samples_all_on(dhidden).reshape(out_count, edge, width)
     chosen = row_grads[outs_idx]
     back_prods = jnp.einsum("tij,tif->tjf", values, chosen, preferred_element_type=jnp.float32)
     sections_part = jnp.einsum("it,tjf->ijf", in_hot, back_prods, precision=lax.Precision.HIGHEST)

time: 225 us -> 208 us (0.924)
  blocking collectives: 15.9 us -> 0 us
    all_gather x1 -> x0, blocking collectives: 15.9 us -> none  [body(): lax.all_gather(dhidden, 'col', axis=0, tiled=True)]
    psum x1, waiting for transfers between devices: 113 us -> 98.2 us  [body(): lax.psum(local_grad, ('row', 'col', 'rep'))]
    ppermute x0 -> x2, waiting for transfers between devices: none -> 14.2 us  [watch_the_waves(): field_out = lax.ppermute(u_next, axis_tag, runs)]
  transfers between devices with their start and end apart: 8 -> 10, of which waited for: 6 -> 6; matrix products, arithmetic and copies ran while one was open for 3% -> 9% of each run, Pallas kernels for 0% -> 0%
where the time goes in v1:
time: 208 us
  waiting for transfers between devices  138 us (66%)
  starting transfers between devices  17.8 us (9%)
  matrix products  17 us (8%)
  between operations  14.9 us (7%)
  local copies, waits for them, and re-layouts  13.4 us (6%)
  other arithmetic  6.38 us (3%)
    psum x1, waiting for transfers between devices, body(): lax.psum(local_grad, ('row', 'col', 'rep'))  98.2 us
    reduce_scatter x1, waiting for transfers between devices, body(): lax.psum_scatter(part.reshape(out_count * edge, width).astype(jnp.bfloat1...  21.4 us
    ppermute x6, starting transfers between devices, passed_along(): lax.ppermute(value, axis, [(source, source + steps) for source in range(l...  16.8 us
    ppermute x2, waiting for transfers between devices, watch_the_waves(): field_out = lax.ppermute(u_next, axis_tag, runs)  14.2 us
    dot_general x1, local copies, waits for them, and re-layouts, body(): jnp.einsum('tij,tif->tjf', values, chosen, preferred_element_type=jnp.flo...  5.53 us
    dot_general x1, local copies, waits for them, and re-layouts, body(): jnp.einsum('tij,tjf->tif', values, picked, preferred_element_type=jnp.flo...  5.51 us
    ppermute x6, waiting for transfers between devices, passed_along(): lax.ppermute(value, axis, [(source, source + steps) for source in range(l...  4.44 us
    dot_general x1, matrix products, body(): jnp.einsum('ot,tif->oif', out_hot, prods, precision=lax.Precision.HIGHEST)  4.34 us
  transfers between devices with their start and end apart: 10, of which 6 were waited for; matrix products, arithmetic and copies ran while one was open for 9% of the time, Pallas kernels for 0%

profile of v1, /device:TPU:0, one launch (start us, length us, event | category | flops | bytes accessed | tf_op | source)
XLA Modules:
  0.0 207.8 jit_solution(5129480842648217826)
XLA Ops:
  7.2 5.0 %collective-permute-start = (bf16[128,512]{1,0:T(8,128)(2,1)}, bf16[128,512]{1,0:T(8,128)(2,1)S(1)}, u32[]{:S(2)}, u32[]{:S(2)}) collective-permute-start(bf16[128,512]{1,0:T(8,128)(2,1)} %bitcast.76), channel_id=1, source_target_pairs={{0,16},{8,24},{1,17},{9,25},{2,18},{10,26},{3,19},{11,27},{4,20},{... | collective-permute-start | bytes 393224 | tf_op jit(solution)/shard_map/ppermute | solution.py:31
  12.2 3.4 %collective-permute-start.1 = (bf16[128,512]{1,0:T(8,128)(2,1)}, bf16[128,512]{1,0:T(8,128)(2,1)S(1)}, u32[]{:S(2)}, u32[]{:S(2)}) collective-permute-start(bf16[128,512]{1,0:T(8,128)(2,1)} %bitcast.77), channel_id=1, source_target_pairs={{0,8},{8,16},{16,24},{1,9},{9,17},{17,25},{2,10},{10,18},{18,26},{... | collective-permute-start | bytes 393224 | tf_op jit(solution)/shard_map/ppermute | solution.py:31
  15.7 1.3 collective-permute-start.2
  18.5 4.3 %collective-permute-done.2 = bf16[128,512]{1,0:T(8,128)(2,1)S(1)} collective-permute-done((bf16[128,512]{1,0:T(8,128)(2,1)}, bf16[128,512]{1,0:T(8,128)(2,1)S(1)}, u32[]{:S(2)}, u32[]{:S(2)}) %collective-permute-start.2) | collective-permute-done | bytes 131104 | tf_op jit(solution)/shard_map/ppermute | solution.py:31
  22.7 1.0 pad_maximum_fusion
  24.4 2.7 %fusion.12 = f32[16,512,128]{2,1,0:T(8,128)} fusion(bf16[16,128,512]{2,1,0:T(8,128)(2,1)S(1)} %gather_fusion, bf16[1,16,128,128]{3,2,1,0:T(8,128)(2,1)S(1)} %copy-done), kind=kOutput, calls=%fused_computation.13 | convolution fusion | flops 268435456 | bytes 6815744 | tf_op jit(solution)/shard_map/tij,tjf->tif/dot_general | solution.py:64
  27.1 5.5 %copy.16 = f32[16,512,128]{1,0,2:T(8,128)} copy(f32[16,512,128]{2,1,0:T(8,128)} %fusion.12) | data formatting | bytes 8388608 | tf_op jit(solution)/shard_map/tij,tjf->tif/dot_general | solution.py:64
  32.7 4.3 %fusion.4 = bf16[4,128,512]{2,0,1:T(4,128)(2,1)S(1)} fusion(f32[16,512,128]{1,0,2:T(8,128)} %copy.16, f32[16]{0:T(128)S(1)} %compare_convert_fusion, s32[16]{0:T(128)S(1)} %bitcast.82), kind=kOutput, calls=%fused_computation.6 | convolution fusion | flops 50593920 | bytes 4718720 | tf_op jit(solution)/shard_map/ot,tif->oif/dot_general | solution.py:65
  37.0 0.9 copy.13
  38.0 21.4 %reduce-scatter.2.cloned.1.call-done = bf16[128,512]{1,0:T(8,128)(2,1)} async-done(((bf16[512,512]{1,0:T(8,128)(2,1)}), bf16[128,512]{1,0:T(8,128)(2,1)}) %reduce-scatter.2.cloned.1.call-update) | async-done | bytes 131088 | tf_op jit(solution)/shard_map/reduce_scatter | solution.py:66
  59.4 1.2 fusion.38
  61.1 4.9 %collective-permute-done.3 = bf16[128,512]{1,0:T(8,128)(2,1)S(1)} collective-permute-done((bf16[128,512]{1,0:T(8,128)(2,1)S(1)}, bf16[128,512]{1,0:T(8,128)(2,1)S(1)}, u32[]{:S(2)}, u32[]{:S(2)}) %collective-permute-start.3) | collective-permute-done | bytes 131104 | tf_op jit(solution)/shard_map/ppermute | solution.py:17
  66.0 0.8 collective-permute-start.4
  66.9 1.3 fusion.34
  68.2 0.7 fusion.19
  69.0 9.3 %collective-permute-done.4 = bf16[256,512]{1,0:T(8,128)(2,1)S(1)} collective-permute-done((bf16[256,512]{1,0:T(8,128)(2,1)S(1)}, bf16[256,512]{1,0:T(8,128)(2,1)S(1)}, u32[]{:S(2)}, u32[]{:S(2)}) %collective-permute-start.4) | collective-permute-done | bytes 262176 | tf_op jit(solution)/shard_map/ppermute | solution.py:17
  79.2 2.7 %fusion.10 = f32[16,512,128]{2,1,0:T(8,128)} fusion(bf16[16,128,512]{2,1,0:T(8,128)(2,1)S(1)} %gather_fusion.1, bf16[1,16,128,128]{3,2,1,0:T(8,128)(2,1)S(1)} %copy-done), kind=kOutput, calls=%fused_computation.11 | convolution fusion | flops 268435456 | bytes 6815744 | tf_op jit(solution)/shard_map/tij,tif->tjf/dot_general | solution.py:86
  81.9 5.5 %copy.17 = f32[16,512,128]{1,0,2:T(8,128)} copy(f32[16,512,128]{2,1,0:T(8,128)} %fusion.10) | data formatting | bytes 8388608 | tf_op jit(solution)/shard_map/tij,tif->tjf/dot_general | solution.py:86
  87.4 4.3 %fusion.7 = bf16[4,128,512]{2,0,1:T(4,128)(2,1)S(1)} fusion(f32[16,512,128]{1,0,2:T(8,128)} %copy.17, s32[16]{0:T(128)S(1)} %bitcast.83, f32[16]{0:T(128)S(1)} %compare_convert_fusion), kind=kOutput, calls=%fused_computation.7 | convolution fusion | flops 50593920 | bytes 4718720 | tf_op jit(solution)/shard_map/it,tjf->ijf/dot_general | solution.py:87
  92.5 1.3 collective-permute-start.5
  93.8 1.3 collective-permute-start.6
  95.2 4.6 %collective-permute-start.7 = (bf16[128,512]{1,0:T(8,128)(2,1)S(1)}, bf16[128,512]{1,0:T(8,128)(2,1)S(1)}, u32[]{:S(2)}, u32[]{:S(2)}) collective-permute-start(bf16[128,512]{1,0:T(8,128)(2,1)S(1)} %bitcast.75), channel_id=1, source_target_pairs={{0,8},{8,16},{16,24},{1,9},{9,17},{17,25},{2,10},{10,18},{18,26},{... | collective-permute-start | bytes 393224 | tf_op jit(solution)/shard_map/ppermute | solution.py:31
  99.7 98.2 %all-reduce.2.cloned.1.call-done = f32[512,512]{1,0:T(8,128)} async-done(((f32[512,512]{1,0:T(8,128)}), f32[512,512]{1,0:T(8,128)}) %all-reduce.2.cloned.1.call-update) | async-done | bytes 1048592 | tf_op jit(solution)/shard_map/psum | solution.py:80
  197.9 2.3 %broadcast_multiply_fusion = f32[512,512]{1,0:T(8,128)} fusion(f32[512,512]{1,0:T(8,128)} %all-reduce.2.cloned.1.call-done), kind=kLoop, calls=%fused_computation.15 | loop fusion | flops 262144 | bytes 2097152 | tf_op jit(solution)/shard_map/mul | solution.py:80
  (37 shorter events, 4.5 us)
Async XLA Ops:
  7.2 17.2 %copy-start = (bf16[1,16,128,128]{3,2,1,0:T(8,128)(2,1)S(1)}, bf16[1,16,128,128]{3,2,1,0:T(8,128)(2,1)}, u32[]{:S(2)}) copy-start(bf16[1,16,128,128]{3,2,1,0:T(8,128)(2,1)} %param.10) | copy-start | bytes 1572868
  7.2 52.2 %reduce-scatter.2.cloned.1.call-start = ((), (), s32[]{:S(2)}) async-start(), calls=%async_computation.1 | async-start | bytes 655360 | tf_op jit(solution)/shard_map/reduce_scatter | solution.py:66
  7.2 11.1 %collective-permute-start = (bf16[128,512]{1,0:T(8,128)(2,1)}, bf16[128,512]{1,0:T(8,128)(2,1)S(1)}, u32[]{:S(2)}, u32[]{:S(2)}) collective-permute-start(bf16[128,512]{1,0:T(8,128)(2,1)} %bitcast.76), channel_id=1, source_target_pairs={{0,16},{8,24},{1,17},{9,25},{2,18},{10,26},{3,19},{11,27},{4,20},{... | collective-permute-start | bytes 393224 | tf_op jit(solution)/shard_map/ppermute | solution.py:31
  12.2 6.2 %collective-permute-start.1 = (bf16[128,512]{1,0:T(8,128)(2,1)}, bf16[128,512]{1,0:T(8,128)(2,1)S(1)}, u32[]{:S(2)}, u32[]{:S(2)}) collective-permute-start(bf16[128,512]{1,0:T(8,128)(2,1)} %bitcast.77), channel_id=1, source_target_pairs={{0,8},{8,16},{16,24},{1,9},{9,17},{17,25},{2,10},{10,18},{18,26},{... | collective-permute-start | bytes 393224 | tf_op jit(solution)/shard_map/ppermute | solution.py:31
  15.7 7.1 %collective-permute-start.2 = (bf16[128,512]{1,0:T(8,128)(2,1)}, bf16[128,512]{1,0:T(8,128)(2,1)S(1)}, u32[]{:S(2)}, u32[]{:S(2)}) collective-permute-start(bf16[128,512]{1,0:T(8,128)(2,1)} %bitcast.78), channel_id=1, source_target_pairs={{8,0},{16,8},{24,16},{9,1},{17,9},{25,17},{10,2},{18,10},{26,18},{... | collective-permute-start | bytes 393224 | tf_op jit(solution)/shard_map/ppermute | solution.py:31
  27.1 5.5 %copy-start.3 = (s32[1,16]{1,0:T(1,128)S(1)}, s32[1,16]{1,0:T(1,128)}, u32[]{:S(2)}) copy-start(s32[1,16]{1,0:T(1,128)} %param.11) | copy-start | bytes 196
  32.7 26.8 %copy-start.1 = (bf16[512,512]{1,0:T(8,128)(2,1)S(1)}, bf16[512,512]{1,0:T(8,128)(2,1)}, u32[]{:S(2)}) copy-start(bf16[512,512]{1,0:T(8,128)(2,1)} %param.9) | copy-start | bytes 1572868
  37.0 23.6 %copy-start.5 = (bf16[1,128,512]{2,1,0:T(8,128)(2,1)S(1)}, bf16[1,128,512]{2,1,0:T(8,128)(2,1)}, u32[]{:S(2)}) copy-start(bf16[1,128,512]{2,1,0:T(8,128)(2,1)} %param.8) | copy-start | bytes 393220
  37.9 160.0 %all-reduce.2.cloned.1.call-start = ((), (), s32[]{:S(2)}) async-start(), calls=%async_computation.2 | async-start | bytes 2097152 | tf_op jit(solution)/shard_map/psum | solution.py:80
  59.4 7.4 %copy-start.2 = (bf16[128,512]{1,0:T(8,128)(2,1)S(1)}, bf16[128,512]{1,0:T(8,128)(2,1)}, u32[]{:S(2)}) copy-start(bf16[128,512]{1,0:T(8,128)(2,1)} %reduce-scatter.2.cloned.1.call-done) | copy-start | bytes 393220
  60.9 5.0 %collective-permute-start.3 = (bf16[128,512]{1,0:T(8,128)(2,1)S(1)}, bf16[128,512]{1,0:T(8,128)(2,1)S(1)}, u32[]{:S(2)}, u32[]{:S(2)}) collective-permute-start(bf16[128,512]{1,0:T(8,128)(2,1)S(1)} %convolution_convert_fusion), channel_id=1, source_target_pairs={{0,2},{2,0},{4,6},{6,4},{1,3},{3,1},{5,7},{7,5},{8,10},{10,8},{12,... | collective-permute-start | bytes 393224 | tf_op jit(solution)/shard_map/ppermute | solution.py:17
  66.0 12.2 %collective-permute-start.4 = (bf16[256,512]{1,0:T(8,128)(2,1)S(1)}, bf16[256,512]{1,0:T(8,128)(2,1)S(1)}, u32[]{:S(2)}, u32[]{:S(2)}) collective-permute-start(bf16[256,512]{1,0:T(8,128)(2,1)S(1)} %maximum_select_fusion.1), channel_id=1, source_target_pairs={{0,4},{2,6},{4,0},{6,2},{1,5},{3,7},{5,1},{7,3},{8,12},{10,14},{12... | collective-permute-start | bytes 786440 | tf_op jit(solution)/shard_map/ppermute | solution.py:17
  81.9 5.5 %copy-start.4 = (s32[1,16]{1,0:T(1,128)S(1)}, s32[1,16]{1,0:T(1,128)}, u32[]{:S(2)}) copy-start(s32[1,16]{1,0:T(1,128)} %param.12) | copy-start | bytes 196
  92.5 107.7 %collective-permute-start.5 = (bf16[128,512]{1,0:T(8,128)(2,1)S(1)}, bf16[128,512]{1,0:T(8,128)(2,1)S(1)}, u32[]{:S(2)}, u32[]{:S(2)}) collective-permute-start(bf16[128,512]{1,0:T(8,128)(2,1)S(1)} %bitcast.73), channel_id=1, source_target_pairs={{16,0},{24,8},{17,1},{25,9},{18,2},{26,10},{19,3},{27,11},{20,4},{... | collective-permute-start | bytes 393224 | tf_op jit(solution)/shard_map/ppermute | solution.py:31
  93.8 106.4 %collective-permute-start.6 = (bf16[128,512]{1,0:T(8,128)(2,1)S(1)}, bf16[128,512]{1,0:T(8,128)(2,1)S(1)}, u32[]{:S(2)}, u32[]{:S(2)}) collective-permute-start(bf16[128,512]{1,0:T(8,128)(2,1)S(1)} %bitcast.74), channel_id=1, source_target_pairs={{8,0},{16,8},{24,16},{9,1},{17,9},{25,17},{10,2},{18,10},{26,18},{... | collective-permute-start | bytes 393224 | tf_op jit(solution)/shard_map/ppermute | solution.py:31
  95.2 105.1 %collective-permute-start.7 = (bf16[128,512]{1,0:T(8,128)(2,1)S(1)}, bf16[128,512]{1,0:T(8,128)(2,1)S(1)}, u32[]{:S(2)}, u32[]{:S(2)}) collective-permute-start(bf16[128,512]{1,0:T(8,128)(2,1)S(1)} %bitcast.75), channel_id=1, source_target_pairs={{0,8},{8,16},{16,24},{1,9},{9,17},{17,25},{2,10},{10,18},{18,26},{... | collective-permute-start | bytes 393224 | tf_op jit(solution)/shard_map/ppermute | solution.py:31
Sparse Core Ops, SparseCore 0:
  38.0 21.3 reduce-scatter.1
  68.3 129.5 all-reduce.1
